TPU v7x, 32 devices: a whole 2x2x4 slice. The times are simulated.
32 devices in a mesh: groups: 2 (over y), clips: 4 (over z), tm: 2 (over x), chan: 2 (over core).
Axes of the slice: x: 2, y: 2, z: 4, core: 2. Of those that a mesh axis runs over, the one named last changes fastest.
Arguments:
- video: bfloat16 [4, 64, 4, 8, 128], P(('groups', 'tm'), 'clips', None, None, 'chan'), parts along dimension 0, may hold values from -6 to 6, as said below
- frame_owner: int32 [4, 64, 1], P(('groups', 'tm'), 'clips'), parts along dimension 0, may hold values from 0 to 3, as said below
- conv_first: bfloat16 [3, 3, 3, 128, 128], replicated, may hold values from -0.109375 to 0.109375
- conv_second: bfloat16 [3, 3, 3, 128, 128], replicated, may hold values from -0.109375 to 0.109375
Outputs:
- encoded: bfloat16 [4, 128, 4, 8, 128], P(('groups', 'tm'), 'clips', None, None, 'chan'), parts along dimension 0
There are 2 independent parts, one for each index of `groups`. A program takes and returns all parts, laid end to end along the dimension named above; an argument that names none is the same for every part. Nothing has to cross between parts.
Inputs may be any that keep to these rules, and one draw needn't show every extreme that they name: `frame_owner`: in each aligned block of 16 rows (the frames of one reader device in one period) no owner is named more than 8 times, and in every block some owner exactly 8 times. A clip may have no frame, or a single frame, in a whole period, and may have no frame over several periods in a row. `video`: A stored frame may be black: all its entries zero.
All inputs are finite; a program needn't handle non-finite values.
Results may differ from a plain program's by a relative error of at most 0.0044.
Values may be sent and summed in bfloat16 or wider, within the bound.
A program may use at most 64 MiB of HBM per device.

v0:
```python
import jax
import jax.numpy as jnp
from jax import lax
from jax.sharding import PartitionSpec as P

EPSILON = 1e-06


def carried_in(part, axis, combine, identity):
    place = lax.axis_index(axis)
    gathered = jax.tree.map(lambda a: lax.all_gather(a, axis), part)
    state = jax.tree.map(lambda a, e: jnp.zeros_like(a) + jnp.asarray(e, a.dtype), part, identity)

    def one(hop, state):
        return combine(
            state, jax.tree.map(lambda a: lax.dynamic_index_in_dim(a, hop, 0, False), gathered)
        )

    return lax.fori_loop(0, place, one, state)


def normalize(values):
    values = values.astype(jnp.float32)
    meansq = jnp.mean(values * values, axis=-1, keepdims=True)
    return jax.nn.silu(values * lax.rsqrt(meansq + EPSILON))


def spatial_conv(frames, weights, offset, length):
    frame_height = frames.shape[1]
    frame_width = frames.shape[2]
    padded_frames = jnp.pad(frames, ((0, 0), (1, 1), (1, 1), (0, 0)))
    accumulated = jnp.zeros((length, frame_height, frame_width, weights.shape[4]), jnp.float32)
    for tap_time in range(weights.shape[0]):
        window = padded_frames[offset - tap_time : offset - tap_time + length]
        for tap_row in range(weights.shape[1]):
            patches = jnp.concatenate(
                [
                    window[:, tap_row : tap_row + frame_height, tap_col : tap_col + frame_width, :]
                    for tap_col in range(weights.shape[2])
                ],
                axis=-1,
            )
            kernel = weights[tap_time, tap_row].reshape(-1, weights.shape[4])
            accumulated = accumulated + jnp.einsum(
                "fhwc,co->fhwo", patches, kernel, preferred_element_type=jnp.float32
            )
    return accumulated


def last_frames(frames, number_live, tail_depth):
    padded_frames = jnp.concatenate(
        [jnp.zeros((tail_depth,) + frames.shape[1:], frames.dtype), frames], axis=0
    )
    return lax.dynamic_slice_in_dim(padded_frames, number_live, tail_depth, 0)


def live_of(number_live, tail_depth):
    return jnp.minimum(number_live, tail_depth).astype(jnp.bfloat16).reshape(1)


def join_tails(earlier, later):
    early_frames, early_live = earlier
    late_frames, late_live = later
    tail_depth = late_frames.shape[0]
    late_used = late_live[0].astype(jnp.int32)
    spread = jnp.concatenate([late_frames, jnp.zeros_like(late_frames)], axis=0)
    leading = lax.dynamic_slice_in_dim(spread, tail_depth - late_used, tail_depth, 0)
    joined = jnp.concatenate([early_frames, leading], axis=0)
    merged_frames = lax.dynamic_slice_in_dim(joined, late_used, tail_depth, 0)
    live_count = jnp.minimum(early_live + late_live, float(tail_depth)).astype(late_live.dtype)
    return (merged_frames, live_count)


def empty_tail(frames, tail_depth):
    return (
        jnp.zeros((tail_depth,) + frames.shape[1:], frames.dtype),
        jnp.zeros((1,), jnp.bfloat16),
    )


def body(video, frame_owner, conv_first, conv_second):
    clip_count = lax.axis_size("clips")
    chan_index = lax.axis_index("chan")
    slot_total = video.shape[1]
    capacity = max(2, 2 * slot_total // clip_count)
    buffer_size = clip_count * capacity
    owners = frame_owner[0, :, 0]
    onehot = (owners[:, None] == jnp.arange(clip_count, dtype=jnp.int32)[None, :]).astype(jnp.int32)
    slot_rank = jnp.sum((jnp.cumsum(onehot, axis=0) - 1) * onehot, axis=1)
    target = owners * capacity + slot_rank
    local_video = video[0]
    outgoing = (
        jnp.zeros((buffer_size,) + local_video.shape[1:], jnp.bfloat16).at[target].set(local_video)
    )
    present = (
        jnp.zeros((buffer_size,), jnp.bfloat16)
        .at[target]
        .set(jnp.ones_like(owners, dtype=jnp.bfloat16))
    )
    outgoing = outgoing.reshape((clip_count, capacity) + local_video.shape[1:])
    present = present.reshape(clip_count, capacity)
    arrived, arrived_mask = (
        lax.all_to_all(outgoing, "clips", split_axis=0, concat_axis=0, tiled=True),
        lax.all_to_all(present, "clips", split_axis=0, concat_axis=0, tiled=True),
    )
    arrived_rows = arrived.reshape((buffer_size,) + arrived.shape[2:])
    is_valid = arrived_mask.reshape(buffer_size).astype(jnp.int32)
    number_live = jnp.sum(is_valid)
    placing = jnp.argsort(1 - is_valid, stable=True)
    inverse = jnp.argsort(placing)
    sorted_rows = arrived_rows[placing]
    frames = lax.all_gather(sorted_rows, "chan", axis=3, tiled=True)
    channel_width = sorted_rows.shape[-1]
    first_local = lax.dynamic_slice_in_dim(conv_first, chan_index * channel_width, channel_width, 4)
    second_local = lax.dynamic_slice_in_dim(
        conv_second, chan_index * channel_width, channel_width, 4
    )
    active = normalize(frames).astype(jnp.bfloat16)
    tail_in, tail_active_count = carried_in(
        (last_frames(active, number_live, 2), live_of(number_live, 2)),
        "tm",
        join_tails,
        empty_tail(active, 2),
    )
    hidden = spatial_conv(
        jnp.concatenate([tail_in, active], axis=0), first_local, 2, buffer_size
    ).astype(jnp.bfloat16)
    hidden_whole = lax.all_gather(hidden, "chan", axis=3, tiled=True)
    second = normalize(hidden_whole).astype(jnp.bfloat16)
    tail_second, second_live = carried_in(
        (last_frames(second, number_live, 2), live_of(number_live, 2)),
        "tm",
        join_tails,
        empty_tail(second, 2),
    )
    update = spatial_conv(
        jnp.concatenate([tail_second, second], axis=0), second_local, 2, buffer_size
    )
    result = (sorted_rows.astype(jnp.float32) + update).astype(jnp.bfloat16)
    placed = result[inverse]
    placed = jnp.where(is_valid[:, None, None, None] > 0, placed, jnp.zeros_like(placed))
    return placed.reshape((1, buffer_size) + placed.shape[1:])


def solution(mesh):
    placed = (
        P(("groups", "tm"), "clips", None, None, "chan"),
        P(("groups", "tm"), "clips", None),
        P(),
        P(),
    )
    return jax.shard_map(
        body,
        mesh=mesh,
        in_specs=placed,
        out_specs=P(("groups", "tm"), "clips", None, None, "chan"),
        check_vma=False,
    )
```

profile of v0, /device:TPU:10, one launch (start us, length us, event | category | flops | bytes accessed | tf_op | source)
XLA Modules:
  0.0 66.3 jit_solution(16387334830662408122)
XLA Ops:
  0.0 0.8 %fusion.115 = s32[16,4]{1,0:T(8,128)S(1)} fusion(s32[16]{0:T(128)} %bitcast.130), kind=kLoop, calls=%fused_computation.210 | loop fusion | flops 128 | bytes 320 | tf_op jit(solution)/shard_map/convert_element_type | solution.py:88
  0.8 0.8 %select_reduce_fusion = s32[16]{0:T(128)S(1)} fusion(s32[16,4]{1,0:T(8,128)S(1)} %reduce_window_sum.11, s32[16]{0:T(128)} %bitcast.131), kind=kLoop, calls=%fused_computation.208 | loop fusion | flops 240 | bytes 384 | tf_op jit(solution)/shard_map/reduce_sum | solution.py:89
  1.7 0.7 %fusion.116 = s32[16]{0:T(128)S(1)} fusion(s32[16]{0:T(128)S(1)} %select_reduce_fusion, s32[1,16,1]{1,2,0:T(1,128)} %param.9), kind=kLoop, calls=%fused_computation.237 | loop fusion | flops 80 | bytes 192 | tf_op jit(solution)/shard_map/select_n | solution.py:98
  2.3 0.7 scatter_custom_fusion
  3.0 0.7 %all_to_all.12 = bf16[4,1,8]{2,1,0:T(2,128)(2,1)} reshape(bf16[32]{0:T(256)(128)(2,1)S(1)} %scatter_custom_fusion) | data formatting | bytes 128 | tf_op jit(solution)/shard_map/all_to_all | solution.py:104
  3.7 5.3 %all-to-all-start = ((bf16[4,1,8]{2,1,0:T(2,128)(2,1)}), bf16[4,1,8]{2,1,0:T(2,128)(2,1)S(1)}, u32[]{:S(2)}, u32[]{:S(2)}) async-start(bf16[4,1,8]{2,1,0:T(2,128)(2,1)} %all_to_all.12), calls=%async_computation | async-start | bytes 4096 | tf_op jit(solution)/shard_map/all_to_all | solution.py:104
  9.1 1.7 %scatter_fusion = bf16[32,4,8,64]{3,2,1,0:T(8,128)(2,1)S(1)} fusion(bf16[32,4,8,64]{3,2,1,0:T(8,128)(2,1)S(1)} %broadcast.129, s32[16]{0:T(128)S(1)} %fusion.116, bf16[16,4,8,64]{3,2,1,0:T(8,128)(2,1)} %bitcast.111), kind=kCustom, calls=%fused_computation.3 | custom fusion | bytes 196672 | tf_op jit(solution)/shard_map/scatter | solution.py:93
  10.8 0.9 %reshape.160 = bf16[4,2,8192]{2,1,0:T(2,128)(2,1)} reshape(bf16[4,8,4,8,64]{4,3,2,1,0:T(8,128)(2,1)S(1)} %bitcast.107) | data formatting | bytes 262144
  11.7 1.0 %constant_dynamic-slice_fusion.19 = (bf16[1,1,3,128,64]{4,3,2,1,0:T(8,128)(2,1)S(1)}, bf16[1,1,3,128,64]{4,3,2,1,0:T(8,128)(2,1)S(1)}, bf16[1,1,3,128,64]{4,3,2,...) fusion(bf16[3,3,3,128,128]{4,3,2,1,0:T(8,128)(2,1)S(1)} %copy-d, ...), kind=kLoop, calls=%fused_computation.229 | loop fusion | bytes 884748 | tf_op jit(solution)/shard_map/slice | solution.py:43
  13.3 0.6 dynamic-slice
  13.9 5.1 %all-to-all-start.1 = ((bf16[4,2,8192]{2,1,0:T(2,128)(2,1)}), bf16[4,2,8192]{2,1,0:T(2,128)(2,1)S(1)}, u32[]{:S(2)}, u32[]{:S(2)}) async-start(bf16[4,2,8192]{2,1,0:T(2,128)(2,1)} %reshape.160), calls=%async_computation.1 | async-start | bytes 262144 | tf_op jit(solution)/shard_map/all_to_all | solution.py:103
  19.0 0.6 subtract_reduce_fusion
  19.7 1.6 %sort.34 = (s32[32]{0:T(128)}, s32[32]{0:T(128)S(1)}) sort(s32[32]{0:T(128)S(1)} %sub.30, s32[32]{0:T(128)S(1)} %iota.12), dimensions={0}, to_apply=%region_4.5 | sort | flops 160 | bytes 512 | tf_op jit(solution)/shard_map/jit(argsort)/sort | solution.py:109
  22.5 0.7 %dynamic-update-slice = bf16[2]{0:T(256)(128)(2,1)S(1)} dynamic-update-slice(bf16[2]{0:T(256)(128)(2,1)S(1)} %broadcast.136, bf16[1]{0:T(256)(128)(2,1)} %bitcast.14, u32[]{:T(128)} %bitcast.15) | dynamic-update-slice | bytes 8
  23.8 5.0 %all-reduce.6 = bf16[2]{0:T(256)(128)(2,1)S(1)} all-reduce(bf16[2]{0:T(256)(128)(2,1)S(1)} %dynamic-update-slice), channel_id=1, replica_groups=mesh['groups'=2,'clips'=4,'tm'=2,'chan'=2] {'tm'}, use_global_device_ids=true, to_apply=%add.6 | all-reduce | flops 2 | bytes 8
  28.8 1.6 %sort.35 = (s32[32]{0:T(128)}, s32[32]{0:T(128)S(1)}) sort(s32[32]{0:T(128)S(1)} %get-tuple-element.175, s32[32]{0:T(128)S(1)} %iota.13), dimensions={0}, to_apply=%region_12.13 | sort | flops 160 | bytes 512 | tf_op jit(solution)/shard_map/jit(argsort)/sort | solution.py:110
  31.4 0.6 gather_fusion
  32.0 0.9 %copy.123 = bf16[32,4,8,64]{0,2,1,3:T(8,128)(2,1)S(1)} copy(bf16[32,4,8,64]{3,2,1,0:T(8,128)(2,1)S(1)} %gather_fusion) | data formatting | bytes 262144 | tf_op jit(solution)/shard_map/gather | solution.py:111
  32.9 2.6 %all-gather = bf16[32,4,8,128]{0,2,1,3:T(8,128)(2,1)S(1)} all-gather(bf16[32,4,8,64]{0,2,1,3:T(8,128)(2,1)S(1)} %copy.123), channel_id=2, replica_groups=mesh['groups'=2,'clips'=4,'tm'=2,'chan'=2] {'chan'}, dimensions={3}, use_global_device_ids=true | all-gather | bytes 393216 | tf_op jit(solution)/shard_map/all_gather | solution.py:112
  35.4 1.3 %copy.124 = bf16[32,4,8,128]{3,2,1,0:T(8,128)(2,1)S(1)} copy(bf16[32,4,8,128]{0,2,1,3:T(8,128)(2,1)S(1)} %all-gather) | data formatting | bytes 524288 | tf_op jit(solution)/shard_map/all_gather | solution.py:112
  37.5 4.4 %all-gather.1 = bf16[4,4,8,128]{3,2,1,0:T(8,128)(2,1)S(1)} all-gather(bf16[2,4,8,128]{3,2,1,0:T(8,128)(2,1)S(1)} %pad_dynamic-slice_fusion.7), channel_id=3, replica_groups=mesh['groups'=2,'clips'=4,'tm'=2,'chan'=2] {'tm'}, dimensions={0}, use_global_device_ids=true | all-gather | bytes 49152 | tf_op jit(solution)/shard_map/all_gather | solution.py:11
  41.9 1.3 %while.28 = (s32[]{:T(128)}, bf16[2,4,8,128]{3,2,1,0:T(8,128)(2,1)S(1)}, s32[]{:T(128)}, bf16[2,2,4,8,128]{4,3,2,1,0:T(8,128)(2,1)S(1)}, bf16[2,1]{1,0:T(2,128)(...) while((s32[]{:T(128)}, bf16[2,4,8,128]{3,2,1,0:T(8,128)(2,1)S(1)}, s32[]{:T(128)}, ...), condition=%wide.region_8.9_spmd, body=%wide.region_7.8_spmd.sunk | while | flops 8205 | bytes 147697 | solution.py:19
  41.9 0.5 constant_dynamic-slice_fusion.22
  43.6 0.8 %pad_slice_fusion.26 = (bf16[32,4,8,128]{3,2,1,0:T(8,128)(2,1)S(1)}, bf16[32,4,8,128]{3,2,1,0:T(8,128)(2,1)S(1)}, bf16[32,4,8,128]{3,2,1,0:T(8,128)(2,1)S(1)}, b...) fusion(bf16[34,4,8,128]{3,2,1,0:T(8,128)(2,1)S(1)} %pad_maximum, ...), kind=kLoop, calls=%fused_computation.42 | loop fusion | bytes 5259264 | tf_op jit(solution)/shard_map/slice | solution.py:38
  44.8 0.5 copy-done.3
  45.7 0.5 copy-done.2
  46.6 0.4 convolution_add_fusion.13
  47.0 0.4 convolution_add_fusion.12
  47.4 0.4 convolution_add_fusion.11
  47.8 0.4 convolution_add_fusion.10
  48.5 0.4 fusion.4
  48.9 0.9 %copy.137 = bf16[32,4,8,64]{0,2,1,3:T(8,128)(2,1)S(1)} copy(bf16[32,4,8,64]{3,2,1,0:T(8,128)(2,1)S(1)} %fusion.4) | data formatting | bytes 262144 | tf_op jit(solution)/shard_map/convert_element_type | solution.py:127
  49.8 2.7 %all_gather.26 = bf16[32,4,8,128]{0,2,1,3:T(8,128)(2,1)S(1)} all-gather(bf16[32,4,8,64]{0,2,1,3:T(8,128)(2,1)S(1)} %copy.137), channel_id=1, replica_groups=mesh['groups'=2,'clips'=4,'tm'=2,'chan'=2] {'chan'}, dimensions={3}, use_global_device_ids=true | all-gather | bytes 393216 | tf_op jit(solution)/shard_map/all_gather | solution.py:128
  52.6 1.3 %copy.138 = bf16[32,4,8,128]{3,2,1,0:T(8,128)(2,1)S(1)} copy(bf16[32,4,8,128]{0,2,1,3:T(8,128)(2,1)S(1)} %all_gather.26) | data formatting | bytes 524288 | tf_op jit(solution)/shard_map/all_gather | solution.py:128
  54.6 4.4 %all-gather.2 = bf16[4,4,8,128]{3,2,1,0:T(8,128)(2,1)S(1)} all-gather(bf16[2,4,8,128]{3,2,1,0:T(8,128)(2,1)S(1)} %pad_dynamic-slice_fusion.6), channel_id=4, replica_groups=mesh['groups'=2,'clips'=4,'tm'=2,'chan'=2] {'tm'}, dimensions={0}, use_global_device_ids=true | all-gather | bytes 49152 | tf_op jit(solution)/shard_map/all_gather | solution.py:11
  59.0 1.3 %while.29 = (s32[]{:T(128)}, bf16[2,4,8,128]{3,2,1,0:T(8,128)(2,1)S(1)}, s32[]{:T(128)}, bf16[2,2,4,8,128]{4,3,2,1,0:T(8,128)(2,1)S(1)}, bf16[2,1]{1,0:T(2,128)(...) while((s32[]{:T(128)}, bf16[2,4,8,128]{3,2,1,0:T(8,128)(2,1)S(1)}, s32[]{:T(128)}, ...), condition=%wide.region_11.12_spmd, body=%wide.region_10.11_spmd.sunk | while | flops 8205 | bytes 147697 | solution.py:19
  59.0 0.5 constant_dynamic-slice_fusion.23
  60.4 0.8 %pad_slice_fusion.2 = (bf16[32,4,8,128]{3,2,1,0:T(8,128)(2,1)S(1)}, bf16[32,4,8,128]{3,2,1,0:T(8,128)(2,1)S(1)}, bf16[32,4,8,128]{3,2,1,0:T(8,128)(2,1)S(1)}, bf...) fusion(bf16[34,4,8,128]{3,2,1,0:T(8,128)(2,1)S(1)} %pad_maximum, ...), kind=kLoop, calls=%fused_computation.18 | loop fusion | bytes 5259264 | tf_op jit(solution)/shard_map/slice | solution.py:38
  61.4 0.4 fusion.51
  61.8 0.4 convolution_add_fusion.7
  62.2 0.4 convolution_add_fusion.6
  62.6 0.4 convolution_add_fusion.5
  63.0 0.4 convolution_add_fusion.4
  63.3 0.4 convolution_add_fusion.3
  63.7 0.4 convolution_add_fusion.2
  64.5 0.4 fusion.3
  64.9 0.6 gather_fusion.1
  65.5 0.8 %bitcast_select_fusion = bf16[1,32,4,8,64]{4,3,2,1,0:T(8,128)(2,1)} fusion(bf16[32,4,8,64]{3,2,1,0:T(8,128)(2,1)S(1)} %gather_fusion.1, pred[32]{0:T(512)(128)(4,1)S(1)} %gt.18), kind=kLoop, calls=%fused_computation.205 | loop fusion | flops 65536 | bytes 262176 | tf_op jit(solution)/shard_map/jit(_where)/select_n | solution.py:141
  (60 shorter events, 5.4 us)
Async XLA Ops:
  0.0 11.7 %copy-start = (bf16[3,3,3,128,128]{4,3,2,1,0:T(8,128)(2,1)S(1)}, bf16[3,3,3,128,128]{4,3,2,1,0:T(8,128)(2,1)}, u32[]{:S(2)}) copy-start(bf16[3,3,3,128,128]{4,3,2,1,0:T(8,128)(2,1)} %param.10) | copy-start | bytes 2654212
  3.7 10.2 %all-to-all-start = ((bf16[4,1,8]{2,1,0:T(2,128)(2,1)}), bf16[4,1,8]{2,1,0:T(2,128)(2,1)S(1)}, u32[]{:S(2)}, u32[]{:S(2)}) async-start(bf16[4,1,8]{2,1,0:T(2,128)(2,1)} %all_to_all.12), calls=%async_computation | async-start | bytes 4096 | tf_op jit(solution)/shard_map/all_to_all | solution.py:104
  10.8 1.9 %copy-start.1 = (bf16[3,3,3,128,128]{4,3,2,1,0:T(8,128)(2,1)S(1)}, bf16[3,3,3,128,128]{4,3,2,1,0:T(8,128)(2,1)}, u32[]{:S(2)}) copy-start(bf16[3,3,3,128,128]{4,3,2,1,0:T(8,128)(2,1)} %param.11) | copy-start | bytes 2654212
  12.7 0.7 copy-start.5
  13.9 17.2 %all-to-all-start.1 = ((bf16[4,2,8192]{2,1,0:T(2,128)(2,1)}), bf16[4,2,8192]{2,1,0:T(2,128)(2,1)S(1)}, u32[]{:S(2)}, u32[]{:S(2)}) async-start(bf16[4,2,8192]{2,1,0:T(2,128)(2,1)} %reshape.160), calls=%async_computation.1 | async-start | bytes 262144 | tf_op jit(solution)/shard_map/all_to_all | solution.py:103
  43.5 0.9 %copy-start.4 = (bf16[1,1,3,128,64]{4,3,2,1,0:T(8,128)(2,1)S(1)}, bf16[1,1,3,128,64]{4,3,2,1,0:T(8,128)(2,1)}, u32[]{:S(2)}) copy-start(bf16[1,1,3,128,64]{4,3,2,1,0:T(8,128)(2,1)} %get-tuple-element.278) | copy-start | bytes 147460
  44.4 0.9 %copy-start.3 = (bf16[1,1,3,128,64]{4,3,2,1,0:T(8,128)(2,1)S(1)}, bf16[1,1,3,128,64]{4,3,2,1,0:T(8,128)(2,1)}, u32[]{:S(2)}) copy-start(bf16[1,1,3,128,64]{4,3,2,1,0:T(8,128)(2,1)} %get-tuple-element.277) | copy-start | bytes 147460
  45.3 0.9 %copy-start.2 = (bf16[1,1,3,128,64]{4,3,2,1,0:T(8,128)(2,1)S(1)}, bf16[1,1,3,128,64]{4,3,2,1,0:T(8,128)(2,1)}, u32[]{:S(2)}) copy-start(bf16[1,1,3,128,64]{4,3,2,1,0:T(8,128)(2,1)} %get-tuple-element.276) | copy-start | bytes 147460
where the time goes:
time: 66.8 us; the launch traced here: 66.3 us
  blocking collectives  19.1 us (29%)
  local copies, waits for them, and re-layouts  17.5 us (26%)
  starting transfers between devices  10.4 us (16%)
  other arithmetic  8.51 us (13%)
  matrix products  6.8 us (10%)
  between operations  2.62 us (4%)
  loops' own time  1.42 us (2%)
    all_gather x2, blocking collectives, carried_in(): gathered = jax.tree.map(lambda a: lax.all_gather(a, axis), part)  8.83 us
    dot_general x18, matrix products, spatial_conv(): jnp.einsum('fhwc,co->fhwo', patches, kernel, preferred_element_type=jnp.f...  6.8 us
    all_to_all x1, starting transfers between devices, body(): lax.all_to_all(present, 'clips', split_axis=0, concat_axis=0, tiled=True)  5.32 us
    all_to_all x1, starting transfers between devices, body(): lax.all_to_all(outgoing, 'clips', split_axis=0, concat_axis=0, tiled=True)  5.09 us
    unnamed x1, blocking collectives  4.95 us
    unnamed x17, local copies, waits for them, and re-layouts  3.86 us
    all_gather x1, blocking collectives, body(): hidden_whole = lax.all_gather(hidden, 'chan', axis=3, tiled=True)  2.74 us
    all_gather x1, blocking collectives, body(): frames = lax.all_gather(sorted_rows, 'chan', axis=3, tiled=True)  2.56 us
  transfers between devices with their start and end apart: 2, of which 0 were waited for; matrix products, arithmetic and copies ran while one was open for 14% of the time, Pallas kernels for 0%

commit v1 on v0

v1 whole, which is shorter than its diff:
```python
import functools

import jax
import jax.numpy as jnp
from jax import lax
from jax.experimental import pallas as pl
from jax.experimental.pallas import tpu as pltpu
from jax.sharding import PartitionSpec as P

EPSILON = 1e-06
MESH = pl.DeviceIdType.MESH
HALO = 4


def each(count, step):
    if count <= 8:
        for i in range(count):
            step(i)
    else:
        lax.fori_loop(0, count, lambda i, c: (step(i), c)[1], 0)


def exchange_kernel(
    sizes, video, owners, own, halo, counts,
    raw, packed, outbox, tailbox, count_row, after, before,
    load_sem, send_sem, tail_send, count_send, recv_sem, count_recv, pass_send, pass_recv,
):
    readers, periods, slots, cap, depth = sizes
    g = lax.axis_index("groups")
    r = lax.axis_index("clips")
    p = lax.axis_index("tm")
    c = lax.axis_index("chan")
    load = pltpu.make_async_copy(video.at[0], raw, load_sem)
    load.start()

    barrier = pltpu.get_barrier_semaphore()

    def greet(i):
        dp, dr = i // readers, i % readers
        pp, rr = lax.rem(p + dp, periods), lax.rem(r + dr, readers)

        @pl.when(i > 0)
        def _():
            pl.semaphore_signal(barrier, inc=1, device_id=(g, rr, pp, c), device_id_type=MESH)

    each(periods * readers, greet)
    pl.semaphore_signal(barrier, inc=1, device_id=(g, r, p, 1 - c), device_id_type=MESH)

    lane = lax.broadcasted_iota(jnp.int32, (1, 128), 1)
    tally = jnp.zeros((1, 128), jnp.int32)
    names = [owners[0, s] for s in range(slots)]
    for s in range(slots):
        tally = tally + jnp.where(lane == names[s], 1, 0)
    count_row[...] = tally
    counts[p * readers + r] = tally

    def tables(o):
        base = o * 32
        n = jnp.int32(slots)
        after[base + slots] = n
        after[base + slots + 1] = n
        for s in reversed(range(slots)):
            n = jnp.where(names[s] == o, s, n)
            after[base + s] = n
        m = jnp.int32(-1)
        before[base] = m
        for s in range(slots):
            m = jnp.where(names[s] == o, s, m)
            before[base + s + 1] = m

    each(readers, tables)

    load.wait()
    for s in range(slots):
        v = raw[s].astype(jnp.float32).reshape(32, 64)
        packed[s] = jnp.concatenate([v[:16], v[16:]], axis=1).astype(jnp.bfloat16)

    def pack(i):
        o = lax.rem(r + i, readers)
        s = after[o * 32]
        for k in range(cap):
            outbox[i, k] = packed[jnp.minimum(s, slots - 1)]
            s = after[o * 32 + s + 1]
        m = before[o * 32 + slots]
        for k in range(depth):
            m = jnp.maximum(m, 0)
            tailbox[i, k] = packed[m]
            m = before[o * 32 + m]

    each(readers, pack)
    mine = pl.ds(r * cap, cap)
    for k in range(cap):
        own[c, r * cap + k] = outbox[0, k]
    pl.semaphore_wait(barrier, periods * readers)

    source = p * readers + r

    def send_own(i):
        o = lax.rem(r + i, readers)
        to = (g, o, p, c)
        return (
            pltpu.make_async_remote_copy(
                outbox.at[i], own.at[c, mine], send_sem.at[i], recv_sem.at[source],
                device_id=to, device_id_type=MESH),
            pltpu.make_async_remote_copy(
                count_row, counts.at[source], count_send.at[i], count_recv.at[source],
                device_id=to, device_id_type=MESH),
        )

    def send_tail(j):
        dp, i = 1 + j // readers, j % readers
        to = (g, lax.rem(r + i, readers), p + dp, c)
        return (
            pltpu.make_async_remote_copy(
                tailbox.at[i], halo.at[c, pl.ds(source * depth, depth)],
                tail_send.at[j], recv_sem.at[source], device_id=to, device_id_type=MESH),
            pltpu.make_async_remote_copy(
                count_row, counts.at[source], count_send.at[readers + j], count_recv.at[source],
                device_id=to, device_id_type=MESH),
        )

    def start_own(i):
        for d in send_own(i + 1):
            d.start()

    def start_tail(j):
        @pl.when(p + 1 + j // readers < periods)
        def _():
            for d in send_tail(j):
                d.start()

    each(readers - 1, start_own)
    each((periods - 1) * readers, start_tail)

    def relay_own(rr):
        part = own.at[c, pl.ds(rr * cap, cap)]
        q = p * readers + rr
        return pltpu.make_async_remote_copy(
            part, part, pass_send.at[q], pass_recv.at[q],
            device_id=(g, r, p, 1 - c), device_id_type=MESH)

    def relay_tail(q):
        part = halo.at[c, pl.ds(q * depth, depth)]
        return pltpu.make_async_remote_copy(
            part, part, pass_send.at[q], pass_recv.at[q],
            device_id=(g, r, p, 1 - c), device_id_type=MESH)

    relay_own(r).start()

    def arrive_own(i):
        rr = lax.rem(r + i + 1, readers)
        q = p * readers + rr
        part = own.at[c, pl.ds(rr * cap, cap)]
        pltpu.make_async_remote_copy(
            part, part, send_sem.at[0], recv_sem.at[q],
            device_id=(g, rr, p, c), device_id_type=MESH).wait_recv()
        relay_own(rr).start()

    def arrive_tail(q):
        @pl.when(q < p * readers)
        def _():
            part = halo.at[c, pl.ds(q * depth, depth)]
            pltpu.make_async_remote_copy(
                part, part, send_sem.at[0], recv_sem.at[q],
                device_id=(g, lax.rem(q, readers), 0, c), device_id_type=MESH).wait_recv()
            relay_tail(q).start()

    each(readers - 1, arrive_own)
    each((periods - 1) * readers, arrive_tail)

    def count_wait(q):
        pltpu.make_async_remote_copy(
            count_row, counts.at[q], count_send.at[0], count_recv.at[q],
            device_id=(g, r, p, 1 - c), device_id_type=MESH).wait_recv()

    def finish_own(i):
        for d in send_own(i + 1):
            d.wait_send()
        count_wait(p * readers + lax.rem(r + i + 1, readers))

    def finish_tail(j):
        @pl.when(p + 1 + j // readers < periods)
        def _():
            for d in send_tail(j):
                d.wait_send()

    def finish_halo(q):
        @pl.when(q < p * readers)
        def _():
            count_wait(q)
            relay_tail(q).wait_send()
            part = halo.at[1 - c, pl.ds(q * depth, depth)]
            pltpu.make_async_remote_copy(
                part, part, pass_send.at[q], pass_recv.at[q],
                device_id=(g, r, p, 1 - c), device_id_type=MESH).wait_recv()

    def finish_relay(rr):
        q = p * readers + rr
        relay_own(rr).wait_send()
        part = own.at[1 - c, pl.ds(rr * cap, cap)]
        pltpu.make_async_remote_copy(
            part, part, pass_send.at[q], pass_recv.at[q],
            device_id=(g, r, p, 1 - c), device_id_type=MESH).wait_recv()

    each(readers - 1, finish_own)
    each((periods - 1) * readers, finish_tail)
    each((periods - 1) * readers, finish_halo)
    each(readers, finish_relay)


def normalize(values):
    meansq = jnp.mean(values * values, axis=-1, keepdims=True)
    v = values * lax.rsqrt(meansq + EPSILON)
    return v / (1.0 + jnp.exp(-v))


def spread(values, target, first, frames):
    x = values.reshape(frames * 4, 8, 128)
    column = lax.broadcasted_iota(jnp.int32, (1, 8, 128), 1)
    shifted = [
        jnp.where(column == 0, 0.0, pltpu.roll(x, 1, 1)),
        x,
        jnp.where(column == 7, 0.0, pltpu.roll(x, 7, 1)),
    ]
    blank = jnp.zeros((frames, 1, 8, 128), jnp.float32)
    rows = pl.ds(first * 32, frames * 32)
    for v in range(3):
        y = shifted[v].reshape(frames, 4, 8, 128)
        lines = [
            jnp.concatenate([blank, y[:, :3]], axis=1),
            y,
            jnp.concatenate([y[:, 1:], blank], axis=1),
        ]
        for u in range(3):
            tap = u * 3 + v
            target[rows, tap * 128 : (tap + 1) * 128] = (
                lines[u].reshape(frames * 32, 128).astype(jnp.bfloat16)
            )


def conv_kernel(sizes, counts, own, halo, first, second, out, x0, taps_a, taps_b, total):
    readers, periods, slots, cap, depth = sizes
    o = lax.axis_index("clips")
    p = lax.axis_index("tm")
    c = lax.axis_index("chan")
    frames = readers * cap

    number = [counts[p * readers + q, 0, o] for q in range(readers)]
    base = [jnp.int32(0)]
    for q in range(readers):
        base.append(base[-1] + number[q])
    live = base[readers]

    def join(a, b, valid):
        a = a.astype(jnp.float32)
        b = b.astype(jnp.float32)
        whole = jnp.concatenate(
            [
                jnp.concatenate([a[:, :64], b[:, :64]], axis=1),
                jnp.concatenate([a[:, 64:], b[:, 64:]], axis=1),
            ],
            axis=0,
        )
        return jnp.where(valid, whole, 0.0)

    where_tail = [jnp.int32(0)] * HALO
    has_tail = [jnp.bool_(False)] * HALO
    seen = jnp.int32(0)
    for q in reversed(range((periods - 1) * readers)):
        n = jnp.where(q < p * readers, counts[q, 0, o], 0)
        for m in range(HALO):
            hit = (seen <= m) & (m < seen + n)
            where_tail[m] = jnp.where(hit, q * depth + m - seen, where_tail[m])
            has_tail[m] = has_tail[m] | hit
        seen = seen + n
    for m in range(HALO):
        at = where_tail[m]
        x0[HALO - 1 - m] = join(halo[0, at], halo[1, at], has_tail[m])
    for j in range(frames):
        at = jnp.int32(j)
        for q in range(1, readers):
            at = jnp.where(j >= base[q], q * cap + j - base[q], at)
        at = jnp.minimum(at, frames - 1)
        x0[HALO + j] = join(own[0, at], own[1, at], j < live)

    def blocks(count, lead):
        yield 0, lead
        for b in range(lead, count, 8):
            yield b, min(8, count - b)

    for at, n in blocks(frames + HALO, HALO):
        spread(normalize(x0[at : at + n].reshape(n * 32, 128)), taps_a, at, n)

    def conv(taps, weights, at, n):
        acc = None
        for t in range(3):
            rows = pl.ds((at + 2 - t) * 32, n * 32)
            part = jnp.dot(taps[rows, :], weights[t], preferred_element_type=jnp.float32)
            acc = part if acc is None else acc + part
        return acc

    for at, n in blocks(frames + 2, 2):
        hidden = conv(taps_a, first, at, n).astype(jnp.bfloat16).astype(jnp.float32)
        spread(normalize(hidden), taps_b, at, n)

    for at in range(0, frames, 8):
        update = conv(taps_b, second, at, 8)
        y = x0[HALO + at : HALO + at + 8].reshape(256, 128) + update
        y = jnp.where(c == 0, y[:, :64], y[:, 64:])
        total[at : at + 8] = y.reshape(8, 32, 64)

    for q in range(readers):
        for k in range(cap):
            y = total[jnp.minimum(base[q] + k, frames - 1)]
            y = jnp.where(k < number[q], y, 0.0)
            out[0, q * cap + k] = y.reshape(4, 8, 64).astype(jnp.bfloat16)


def body(video, frame_owner, conv_first, conv_second):
    readers = lax.axis_size("clips")
    periods = lax.axis_size("tm")
    slots = video.shape[1]
    cap = max(2, 2 * slots // readers)
    depth = min(HALO, cap)
    frames = readers * cap
    sizes = (readers, periods, slots, cap, depth)
    sources = periods * readers
    vmem = pl.BlockSpec(memory_space=pltpu.VMEM)
    smem = pl.BlockSpec(memory_space=pltpu.SMEM)
    anywhere = pl.BlockSpec(memory_space=pl.ANY)
    dma = pltpu.SemaphoreType.DMA
    own, halo, counts = pl.pallas_call(
        functools.partial(exchange_kernel, sizes),
        out_shape=(
            jax.ShapeDtypeStruct((2, frames, 16, 128), jnp.bfloat16),
            jax.ShapeDtypeStruct((2, (periods - 1) * readers * depth, 16, 128), jnp.bfloat16),
            jax.ShapeDtypeStruct((sources, 1, 128), jnp.int32),
        ),
        in_specs=[anywhere, smem],
        out_specs=(vmem, vmem, vmem),
        scratch_shapes=[
            pltpu.VMEM((slots, 4, 8, 64), jnp.bfloat16),
            pltpu.VMEM((slots, 16, 128), jnp.bfloat16),
            pltpu.VMEM((readers, cap, 16, 128), jnp.bfloat16),
            pltpu.VMEM((readers, depth, 16, 128), jnp.bfloat16),
            pltpu.VMEM((1, 128), jnp.int32),
            pltpu.SMEM((readers * 32,), jnp.int32),
            pltpu.SMEM((readers * 32,), jnp.int32),
            dma,
            dma((readers,)),
            dma((sources,)),
            dma((sources,)),
            dma((sources,)),
            dma((sources,)),
            dma((sources,)),
            dma((sources,)),
        ],
        compiler_params=pltpu.CompilerParams(
            collective_id=0, has_side_effects=True, vmem_limit_bytes=24 * 2**20
        ),
    )(video, frame_owner.reshape(1, slots))

    return pl.pallas_call(
        functools.partial(conv_kernel, sizes),
        out_shape=jax.ShapeDtypeStruct((1, frames, 4, 8, 64), jnp.bfloat16),
        in_specs=[smem, vmem, vmem, vmem, vmem],
        out_specs=vmem,
        scratch_shapes=[
            pltpu.VMEM((frames + HALO, 32, 128), jnp.float32),
            pltpu.VMEM(((frames + HALO) * 32, 1152), jnp.bfloat16),
            pltpu.VMEM(((frames + 2) * 32, 1152), jnp.bfloat16),
            pltpu.VMEM((frames, 32, 64), jnp.float32),
        ],
        compiler_params=pltpu.CompilerParams(vmem_limit_bytes=32 * 2**20),
    )(counts, own, halo, conv_first.reshape(3, 1152, 128), conv_second.reshape(3, 1152, 128))


def solution(mesh):
    placed = (
        P(("groups", "tm"), "clips", None, None, "chan"),
        P(("groups", "tm"), "clips", None),
        P(),
        P(),
    )
    return jax.shard_map(
        body,
        mesh=mesh,
        in_specs=placed,
        out_specs=P(("groups", "tm"), "clips", None, None, "chan"),
        check_vma=False,
    )
```

time: 66.8 us -> 22.6 us (0.34)
  the two profiles are of different devices: /device:TPU:10 before, /device:TPU:1 now
where the time goes in v1:
time: 22.6 us; the launch traced here: 22.3 us
  Pallas kernels  18.4 us (81%)
  local copies, waits for them, and re-layouts  3.89 us (17%)
    pallas_call x1, Pallas kernels, body(): pl.pallas_call(functools.partial(exchange_kernel, sizes), out_shape=(jax....  12.2 us
    pallas_call x1, Pallas kernels, body(): pl.pallas_call(functools.partial(conv_kernel, sizes), out_shape=jax.Shape...  6.2 us
    unnamed x8, local copies, waits for them, and re-layouts  3.89 us

profile of v1, /device:TPU:1, one launch (start us, length us, event | category | flops | bytes accessed | tf_op | source)
XLA Modules:
  0.0 22.3 jit_solution(7863425051647046988)
XLA Ops:
  0.0 0.0 copy-start.3
  0.0 0.7 %copy-done.3 = s32[1,16,1]{1,2,0:T(1,128)S(1)} copy-done((s32[1,16,1]{1,2,0:T(1,128)S(1)}, s32[1,16,1]{1,2,0:T(1,128)}, u32[]{:S(2)}) %copy-start.3) | copy-done | bytes 88
  0.7 0.0 copy-start.2
  0.7 0.9 %copy-done.2 = bf16[1,16,4,8,64]{4,3,2,1,0:T(8,128)(2,1)S(1)} copy-done((bf16[1,16,4,8,64]{4,3,2,1,0:T(8,128)(2,1)S(1)}, bf16[1,16,4,8,64]{4,3,2,1,0:T(8,128)(2,1)}, u32[]{:S(2)}) %copy-start.2) | copy-done | bytes 65560
  1.6 12.2 %shard_map.46 = (bf16[2,32,16,128]{3,2,1,0:T(8,128)(2,1)S(1)}, bf16[2,16,16,128]{3,2,1,0:T(8,128)(2,1)S(1)}, s32[8,1,128]{2,1,0:T(1,128)S(1)}) custom-call(bf16[1,16,4,8,64]{4,3,2,1,0:T(8,128)(2,1)S(1)} %copy-done.2, s32[1,16]{1,0:T(1,128)S(1)} %bitcast.5), custom_call_target="tpu_custom_call" | custom-call | tf_op jit(solution)/shard_map/pallas_call | solution.py:332
  13.8 0.0 copy-start
  13.8 1.2 %copy-done = bf16[3,3,3,128,128]{4,3,2,1,0:T(8,128)(2,1)S(1)} copy-done((bf16[3,3,3,128,128]{4,3,2,1,0:T(8,128)(2,1)S(1)}, bf16[3,3,3,128,128]{4,3,2,1,0:T(8,128)(2,1)}, u32[]{:S(2)}) %copy-start) | copy-done | bytes 884760
  14.9 0.0 copy-start.1
  15.0 1.2 %copy-done.1 = bf16[3,3,3,128,128]{4,3,2,1,0:T(8,128)(2,1)S(1)} copy-done((bf16[3,3,3,128,128]{4,3,2,1,0:T(8,128)(2,1)S(1)}, bf16[3,3,3,128,128]{4,3,2,1,0:T(8,128)(2,1)}, u32[]{:S(2)}) %copy-start.1) | copy-done | bytes 884760
  16.1 6.2 %shard_map.47 = bf16[1,32,4,8,64]{4,3,2,1,0:T(8,128)(2,1)} custom-call(s32[8,1,128]{2,1,0:T(1,128)S(1)} %get-tuple-element.8.counts, bf16[2,32,16,128]{3,2,1,0:T(8,128)(2,1)S(1)} %get-tuple-element.9.own, bf16[2,16,16,128]{3,2,1,0:T(8,128)(2,1)S(1)} %get-tuple-element.10.halo, bf16[3,1152,128]{2,1,0:T(8,128)(2,1)S(1)} %bitcast.3, ...), custom_call_target="tpu_custom_call" | custom-call | tf_op jit(solution)/shard_map/pallas_call | solution.py:363
Async XLA Ops:
  0.0 0.7 %copy-start.3 = (s32[1,16,1]{1,2,0:T(1,128)S(1)}, s32[1,16,1]{1,2,0:T(1,128)}, u32[]{:S(2)}) copy-start(s32[1,16,1]{1,2,0:T(1,128)} %param.5) | copy-start | bytes 196
  0.7 0.9 %copy-start.2 = (bf16[1,16,4,8,64]{4,3,2,1,0:T(8,128)(2,1)S(1)}, bf16[1,16,4,8,64]{4,3,2,1,0:T(8,128)(2,1)}, u32[]{:S(2)}) copy-start(bf16[1,16,4,8,64]{4,3,2,1,0:T(8,128)(2,1)} %video.1) | copy-start | bytes 196612
  13.8 1.2 %copy-start = (bf16[3,3,3,128,128]{4,3,2,1,0:T(8,128)(2,1)S(1)}, bf16[3,3,3,128,128]{4,3,2,1,0:T(8,128)(2,1)}, u32[]{:S(2)}) copy-start(bf16[3,3,3,128,128]{4,3,2,1,0:T(8,128)(2,1)} %param.6) | copy-start | bytes 2654212
  14.9 1.2 %copy-start.1 = (bf16[3,3,3,128,128]{4,3,2,1,0:T(8,128)(2,1)S(1)}, bf16[3,3,3,128,128]{4,3,2,1,0:T(8,128)(2,1)}, u32[]{:S(2)}) copy-start(bf16[3,3,3,128,128]{4,3,2,1,0:T(8,128)(2,1)} %param.7) | copy-start | bytes 2654212

commit v2 on v1

--- a/solution.py
+++ b/solution.py
@@ -20,10 +20,11 @@
         lax.fori_loop(0, count, lambda i, c: (step(i), c)[1], 0)
 
 
-def exchange_kernel(
-    sizes, video, owners, own, halo, counts,
-    raw, packed, outbox, tailbox, count_row, after, before,
-    load_sem, send_sem, tail_send, count_send, recv_sem, count_recv, pass_send, pass_recv,
+def block_kernel(
+    sizes, video, owner_rows, first_in, second_in, out,
+    own, halo, counts, first, second, known, x0, taps_a, taps_b, total,
+    owners, raw, packed, outbox, tailbox, count_row, after, before,
+    known_sem, load_sem, owner_sem, weight_sem, send_sem, tail_send, count_send, recv_sem, count_recv, pass_send, pass_recv,
 ):
     readers, periods, slots, cap, depth = sizes
     g = lax.axis_index("groups")
@@ -31,7 +32,13 @@
     p = lax.axis_index("tm")
     c = lax.axis_index("chan")
     load = pltpu.make_async_copy(video.at[0], raw, load_sem)
+    name_load = pltpu.make_async_copy(owner_rows, owners, owner_sem)
+    name_load.start()
     load.start()
+    weight_loads = [
+        pltpu.make_async_copy(first_in, first, weight_sem.at[0]),
+        pltpu.make_async_copy(second_in, second, weight_sem.at[1]),
+    ]
 
     barrier = pltpu.get_barrier_semaphore()
 
@@ -46,6 +53,9 @@
     each(periods * readers, greet)
     pl.semaphore_signal(barrier, inc=1, device_id=(g, r, p, 1 - c), device_id_type=MESH)
 
+    for d in weight_loads:
+        d.start()
+    name_load.wait()
     lane = lax.broadcasted_iota(jnp.int32, (1, 128), 1)
     tally = jnp.zeros((1, 128), jnp.int32)
     names = [owners[0, s] for s in range(slots)]
@@ -147,6 +157,24 @@
 
     relay_own(r).start()
 
+    def count_wait(q):
+        pltpu.make_async_remote_copy(
+            count_row, counts.at[q], count_send.at[0], count_recv.at[q],
+            device_id=(g, r, p, 1 - c), device_id_type=MESH).wait_recv()
+
+    def count_own(i):
+        count_wait(p * readers + lax.rem(r + i + 1, readers))
+
+    def count_tail(q):
+        @pl.when(q < p * readers)
+        def _():
+            count_wait(q)
+
+    each(readers - 1, count_own)
+    each((periods - 1) * readers, count_tail)
+    known_copy = pltpu.make_async_copy(counts, known, known_sem)
+    known_copy.start()
+
     def arrive_own(i):
         rr = lax.rem(r + i + 1, readers)
         q = p * readers + rr
@@ -168,15 +196,9 @@
     each(readers - 1, arrive_own)
     each((periods - 1) * readers, arrive_tail)
 
-    def count_wait(q):
-        pltpu.make_async_remote_copy(
-            count_row, counts.at[q], count_send.at[0], count_recv.at[q],
-            device_id=(g, r, p, 1 - c), device_id_type=MESH).wait_recv()
-
     def finish_own(i):
         for d in send_own(i + 1):
             d.wait_send()
-        count_wait(p * readers + lax.rem(r + i + 1, readers))
 
     def finish_tail(j):
         @pl.when(p + 1 + j // readers < periods)
@@ -187,21 +209,31 @@
     def finish_halo(q):
         @pl.when(q < p * readers)
         def _():
-            count_wait(q)
             relay_tail(q).wait_send()
+
+    def get_halo(q):
+        @pl.when(q < p * readers)
+        def _():
             part = halo.at[1 - c, pl.ds(q * depth, depth)]
             pltpu.make_async_remote_copy(
                 part, part, pass_send.at[q], pass_recv.at[q],
                 device_id=(g, r, p, 1 - c), device_id_type=MESH).wait_recv()
 
     def finish_relay(rr):
+        relay_own(rr).wait_send()
+
+    def get_relay(rr):
         q = p * readers + rr
-        relay_own(rr).wait_send()
         part = own.at[1 - c, pl.ds(rr * cap, cap)]
         pltpu.make_async_remote_copy(
             part, part, pass_send.at[q], pass_recv.at[q],
             device_id=(g, r, p, 1 - c), device_id_type=MESH).wait_recv()
 
+    each((periods - 1) * readers, get_halo)
+    each(readers, get_relay)
+    known_copy.wait()
+    weight_loads[0].wait()
+    convolve(sizes, known, own, halo, first, second, weight_loads[1], out, x0, taps_a, taps_b, total)
     each(readers - 1, finish_own)
     each((periods - 1) * readers, finish_tail)
     each((periods - 1) * readers, finish_halo)
@@ -238,7 +270,7 @@
             )
 
 
-def conv_kernel(sizes, counts, own, halo, first, second, out, x0, taps_a, taps_b, total):
+def convolve(sizes, counts, own, halo, first, second, second_load, out, x0, taps_a, taps_b, total):
     readers, periods, slots, cap, depth = sizes
     o = lax.axis_index("clips")
     p = lax.axis_index("tm")
@@ -303,6 +335,7 @@
         hidden = conv(taps_a, first, at, n).astype(jnp.bfloat16).astype(jnp.float32)
         spread(normalize(hidden), taps_b, at, n)
 
+    second_load.wait()
     for at in range(0, frames, 8):
         update = conv(taps_b, second, at, 8)
         y = x0[HALO + at : HALO + at + 8].reshape(256, 128) + update
@@ -326,19 +359,25 @@
     sizes = (readers, periods, slots, cap, depth)
     sources = periods * readers
     vmem = pl.BlockSpec(memory_space=pltpu.VMEM)
-    smem = pl.BlockSpec(memory_space=pltpu.SMEM)
-    anywhere = pl.BlockSpec(memory_space=pl.ANY)
+    hbm = pl.BlockSpec(memory_space=pltpu.HBM)
     dma = pltpu.SemaphoreType.DMA
-    own, halo, counts = pl.pallas_call(
-        functools.partial(exchange_kernel, sizes),
-        out_shape=(
-            jax.ShapeDtypeStruct((2, frames, 16, 128), jnp.bfloat16),
-            jax.ShapeDtypeStruct((2, (periods - 1) * readers * depth, 16, 128), jnp.bfloat16),
-            jax.ShapeDtypeStruct((sources, 1, 128), jnp.int32),
-        ),
-        in_specs=[anywhere, smem],
-        out_specs=(vmem, vmem, vmem),
+    return pl.pallas_call(
+        functools.partial(block_kernel, sizes),
+        out_shape=jax.ShapeDtypeStruct((1, frames, 4, 8, 64), jnp.bfloat16),
+        in_specs=[hbm] * 4,
+        out_specs=vmem,
         scratch_shapes=[
+            pltpu.VMEM((2, frames, 16, 128), jnp.bfloat16),
+            pltpu.VMEM((2, (periods - 1) * readers * depth, 16, 128), jnp.bfloat16),
+            pltpu.VMEM((sources, 1, 128), jnp.int32),
+            pltpu.VMEM((3, 1152, 128), jnp.bfloat16),
+            pltpu.VMEM((3, 1152, 128), jnp.bfloat16),
+            pltpu.SMEM((sources, 1, 128), jnp.int32),
+            pltpu.VMEM((frames + HALO, 32, 128), jnp.float32),
+            pltpu.VMEM(((frames + HALO) * 32, 1152), jnp.bfloat16),
+            pltpu.VMEM(((frames + 2) * 32, 1152), jnp.bfloat16),
+            pltpu.VMEM((frames, 32, 64), jnp.float32),
+            pltpu.SMEM((1, slots), jnp.int32),
             pltpu.VMEM((slots, 4, 8, 64), jnp.bfloat16),
             pltpu.VMEM((slots, 16, 128), jnp.bfloat16),
             pltpu.VMEM((readers, cap, 16, 128), jnp.bfloat16),
@@ -347,6 +386,9 @@
             pltpu.SMEM((readers * 32,), jnp.int32),
             pltpu.SMEM((readers * 32,), jnp.int32),
             dma,
+            dma,
+            dma,
+            dma((2,)),
             dma((readers,)),
             dma((sources,)),
             dma((sources,)),
@@ -356,23 +398,14 @@
             dma((sources,)),
         ],
         compiler_params=pltpu.CompilerParams(
-            collective_id=0, has_side_effects=True, vmem_limit_bytes=24 * 2**20
+            collective_id=0, has_side_effects=True, vmem_limit_bytes=60 * 2**20
         ),
-    )(video, frame_owner.reshape(1, slots))
-
-    return pl.pallas_call(
-        functools.partial(conv_kernel, sizes),
-        out_shape=jax.ShapeDtypeStruct((1, frames, 4, 8, 64), jnp.bfloat16),
-        in_specs=[smem, vmem, vmem, vmem, vmem],
-        out_specs=vmem,
-        scratch_shapes=[
-            pltpu.VMEM((frames + HALO, 32, 128), jnp.float32),
-            pltpu.VMEM(((frames + HALO) * 32, 1152), jnp.bfloat16),
-            pltpu.VMEM(((frames + 2) * 32, 1152), jnp.bfloat16),
-            pltpu.VMEM((frames, 32, 64), jnp.float32),
-        ],
-        compiler_params=pltpu.CompilerParams(vmem_limit_bytes=32 * 2**20),
-    )(counts, own, halo, conv_first.reshape(3, 1152, 128), conv_second.reshape(3, 1152, 128))
+    )(
+        video,
+        frame_owner.reshape(1, slots),
+        conv_first.reshape(3, 1152, 128),
+        conv_second.reshape(3, 1152, 128),
+    )
 
 
 def solution(mesh):

time: 22.6 us -> 19.2 us (0.85)
  local copies, waits for them, and re-layouts: 3.89 us -> 1.67 us
  Pallas kernels: 18.4 us -> 17.3 us
    unnamed x8 -> x1, local copies, waits for them, and re-layouts: 3.89 us -> 1.67 us
    pallas_call x2 -> x1, Pallas kernels: 18.4 us -> 17.3 us  [body(): pl.pallas_call(functools.partial(block_kernel, sizes), out_shape=jax.Shap...]
where the time goes in v2:
time: 19.2 us; the launch traced here: 19 us
  Pallas kernels  17.3 us (90%)
  local copies, waits for them, and re-layouts  1.67 us (9%)
    pallas_call x1, Pallas kernels, body(): pl.pallas_call(functools.partial(block_kernel, sizes), out_shape=jax.Shap...  17.3 us
    unnamed x1, local copies, waits for them, and re-layouts  1.67 us

profile of v2, /device:TPU:1, one launch (start us, length us, event | category | flops | bytes accessed | tf_op | source)
XLA Modules:
  0.0 19.0 jit_solution(9087511865167307951)
XLA Ops:
  0.0 17.3 %shard_map.46 = bf16[1,32,4,8,64]{4,3,2,1,0:T(8,128)(2,1)} custom-call(bf16[1,16,4,8,64]{4,3,2,1,0:T(8,128)(2,1)} %video.1, s32[1,16]{1,0:T(1,128)} %bitcast.5, bf16[3,1152,128]{2,1,0:T(8,128)(2,1)} %bitcast.3, bf16[3,1152,128]{2,1,0:T(8,128)(2,1)} %bitcast.4), custom_call_target="tpu_custom_call" | custom-call | tf_op jit(solution)/shard_map/pallas_call | solution.py:364
  17.3 1.7 %copy.6 = bf16[1,32,4,8,64]{4,3,2,1,0:T(8,128)(2,1)} copy(bf16[1,32,4,8,64]{4,3,2,1,0:T(8,128)(2,1)} %shard_map.46) | data formatting | bytes 262144

commit v3 on v2

v3 whole, which is shorter than its diff:
```python
import functools

import jax
import jax.numpy as jnp
from jax import lax
from jax.experimental import pallas as pl
from jax.experimental.pallas import tpu as pltpu
from jax.sharding import PartitionSpec as P

EPSILON = 1e-06
MESH = pl.DeviceIdType.MESH
HALO = 4


def each(count, step):
    if count <= 8:
        for i in range(count):
            step(i)
    else:
        lax.fori_loop(0, count, lambda i, c: (step(i), c)[1], 0)


def block_kernel(
    sizes, video, owner_rows, first_in, second_in, out,
    box, other, tail_in, tail_out, counts, known, first, second, x0, taps_a, taps_b, total,
    owners, raw, packed, after,
    known_sem, load_sem, owner_sem, weight_sem, send_sem, recv_sem, count_send, count_recv,
    pass_send, pass_recv, tail_send, tail_recv,
):
    readers, periods, slots, cap = sizes
    frames = readers * cap
    g = lax.axis_index("groups")
    r = lax.axis_index("clips")
    p = lax.axis_index("tm")
    c = lax.axis_index("chan")
    load = pltpu.make_async_copy(video.at[0], raw, load_sem)
    name_load = pltpu.make_async_copy(owner_rows, owners, owner_sem)
    name_load.start()
    load.start()
    weight_loads = [
        pltpu.make_async_copy(first_in, first, weight_sem.at[0]),
        pltpu.make_async_copy(second_in, second, weight_sem.at[1]),
    ]
    up = (g, r + 1, p, c)
    down = (g, r - 1, p, c)
    later = (g, r, p + 1, c)
    earlier = (g, r, p - 1, c)
    sibling = (g, r, p, 1 - c)

    barrier = pltpu.get_barrier_semaphore()

    def greet(there, who):
        @pl.when(there)
        def _():
            pl.semaphore_signal(barrier, inc=1, device_id=who, device_id_type=MESH)

    greet(r < readers - 1, up)
    greet(r > 0, down)
    greet(p < periods - 1, later)
    greet(p > 0, earlier)
    pl.semaphore_signal(barrier, inc=1, device_id=sibling, device_id_type=MESH)
    for d in weight_loads:
        d.start()

    name_load.wait()
    lane = lax.broadcasted_iota(jnp.int32, (1, 128), 1)
    tally = jnp.zeros((1, 128), jnp.int32)
    names = [owners[0, s] for s in range(slots)]
    for s in range(slots):
        tally = tally + jnp.where(lane == names[s], 1, 0)
    counts[r] = tally

    def tables(o):
        base = o * 32
        n = jnp.int32(slots)
        after[base + slots] = n
        after[base + slots + 1] = n
        for s in reversed(range(slots)):
            n = jnp.where(names[s] == o, s, n)
            after[base + s] = n

    each(readers, tables)

    load.wait()
    for s in range(slots):
        v = raw[s].astype(jnp.float32).reshape(32, 64)
        packed[s] = jnp.concatenate([v[:16], v[16:]], axis=1).astype(jnp.bfloat16)

    def pack(o):
        s = after[o * 32]
        for k in range(cap):
            box[r, o, k] = packed[jnp.minimum(s, slots - 1)]
            s = after[o * 32 + s + 1]

    each(readers, pack)
    neighbours = (
        1
        + jnp.where(r < readers - 1, 1, 0)
        + jnp.where(r > 0, 1, 0)
        + jnp.where(p < periods - 1, 1, 0)
        + jnp.where(p > 0, 1, 0)
    )
    pl.semaphore_wait(barrier, neighbours)

    def remote(source, target, sent, got, who):
        return pltpu.make_async_remote_copy(
            source, target, sent, got, device_id=who, device_id_type=MESH)

    def chunk(s, d, who):
        at = s * readers + d
        return remote(box.at[s, d], box.at[s, d], send_sem.at[at], recv_sem.at[at], who)

    def row(s, way, who):
        return remote(
            counts.at[s], counts.at[s], count_send.at[2 * s + way], count_recv.at[s], who)

    def relay(s):
        return remote(box.at[s, r], other.at[s], pass_send.at[s], pass_recv.at[s], sibling)

    def when(there, act):
        @pl.when(there)
        def _():
            act()

    def start_rows():
        when(r < readers - 1, lambda: row(r, 0, up).start())
        when(r > 0, lambda: row(r, 1, down).start())

    def start_chunks(i):
        d = readers - 1 - i
        when(d > r, lambda: chunk(r, d, up).start())
        when(i < r, lambda: chunk(r, i, down).start())

    each(readers, start_chunks)
    start_rows()
    relay(r).start()

    def arrive(i):
        below, above = r - 1 - i, r + 1 + i

        def from_below(j):
            d = readers - 1 - j

            def take():
                chunk(below, d, up).wait_recv()
                when(d > r, lambda: chunk(below, d, up).start())
                when(d == r, lambda: relay(below).start())

            when((below >= 0) & (d >= r), take)

        def from_above(d):
            def take():
                chunk(above, d, down).wait_recv()
                when(d < r, lambda: chunk(above, d, down).start())
                when(d == r, lambda: relay(above).start())

            when((above < readers) & (d <= r), take)

        def row_below():
            row(below, 0, up).wait_recv()
            when(r < readers - 1, lambda: row(below, 0, up).start())

        def row_above():
            row(above, 1, down).wait_recv()
            when(r > 0, lambda: row(above, 1, down).start())

        def both(j):
            from_below(j)
            from_above(j)

        each(readers, both)
        when(below >= 0, row_below)
        when(above < readers, row_above)

    each(readers - 1, arrive)
    known_copy = pltpu.make_async_copy(counts, known, known_sem)
    known_copy.start()
    each(readers, lambda s: relay(s).wait_recv())
    known_copy.wait()

    number = [known[q, 0, r] for q in range(readers)]
    base = [jnp.int32(0)]
    for q in range(readers):
        base.append(base[-1] + number[q])
    live = jnp.minimum(base[readers], frames)

    x0[:HALO] = jnp.zeros((HALO, 32, 128), jnp.float32)
    for j in range(frames):
        of, at = jnp.int32(0), jnp.int32(j)
        for q in range(1, readers):
            past = j >= base[q]
            of = jnp.where(past, q, of)
            at = jnp.where(past, j - base[q], at)
        at = jnp.minimum(at, cap - 1)
        mine = box[of, r, at].astype(jnp.float32)
        theirs = other[of, at].astype(jnp.float32)
        a = jnp.where(c == 0, mine, theirs)
        b = jnp.where(c == 0, theirs, mine)
        whole = jnp.concatenate(
            [
                jnp.concatenate([a[:, :64], b[:, :64]], axis=1),
                jnp.concatenate([a[:, 64:], b[:, 64:]], axis=1),
            ],
            axis=0,
        )
        x0[HALO + j] = jnp.where(j < live, whole, 0.0)

    carry = remote(tail_out, tail_in, tail_send, tail_recv, later)

    def take_tail():
        carry.wait_recv()
        x0[:HALO] = tail_in[...].astype(jnp.float32)

    def give_tail():
        when(p > 0, take_tail)
        for i in range(HALO):
            tail_out[i] = x0[live + i].astype(jnp.bfloat16)
        carry.start()

    when(p < periods - 1, give_tail)

    def conv(taps, weights, at, n):
        acc = None
        for t in range(3):
            rows = pl.ds((at + 2 - t) * 32, n * 32)
            part = jnp.dot(taps[rows, :], weights[t], preferred_element_type=jnp.float32)
            acc = part if acc is None else acc + part
        return acc

    def enter(at, n):
        spread(normalize(x0[at : at + n].reshape(n * 32, 128)), taps_a, at, n)

    def middle(at, n):
        hidden = conv(taps_a, first, at, n).astype(jnp.bfloat16).astype(jnp.float32)
        spread(normalize(hidden), taps_b, at, n)

    for at in range(HALO, HALO + frames, 8):
        enter(at, 8)
    weight_loads[0].wait()
    at = 4
    while at < frames + 2:
        n = min(frames + 2 - at, 6 if at == 4 else 8)
        middle(at, n)
        at += n
    when(p == periods - 1, take_tail)
    enter(0, HALO)
    middle(0, 4)

    weight_loads[1].wait()
    for at in range(0, frames, 8):
        update = conv(taps_b, second, at, 8)
        y = x0[HALO + at : HALO + at + 8].reshape(256, 128) + update
        y = jnp.where(c == 0, y[:, :64], y[:, 64:])
        total[at : at + 8] = y.reshape(8, 32, 64)

    for q in range(readers):
        for k in range(cap):
            y = total[jnp.minimum(base[q] + k, frames - 1)]
            y = jnp.where(k < number[q], y, 0.0)
            out[0, q * cap + k] = y.reshape(4, 8, 64).astype(jnp.bfloat16)

    def sent(s):
        def one(d):
            when((s <= r) & (d > r), lambda: chunk(s, d, up).wait_send())
            when((s >= r) & (d < r), lambda: chunk(s, d, down).wait_send())

        each(readers, one)
        when((s <= r) & (r < readers - 1), lambda: row(s, 0, up).wait_send())
        when((s >= r) & (r > 0), lambda: row(s, 1, down).wait_send())
        relay(s).wait_send()

    each(readers, sent)
    when(p < periods - 1, carry.wait_send)


def normalize(values):
    meansq = jnp.mean(values * values, axis=-1, keepdims=True)
    v = values * lax.rsqrt(meansq + EPSILON)
    return v / (1.0 + jnp.exp(-v))


def spread(values, target, first, frames):
    x = values.reshape(frames * 4, 8, 128)
    column = lax.broadcasted_iota(jnp.int32, (1, 8, 128), 1)
    shifted = [
        jnp.where(column == 0, 0.0, pltpu.roll(x, 1, 1)),
        x,
        jnp.where(column == 7, 0.0, pltpu.roll(x, 7, 1)),
    ]
    blank = jnp.zeros((frames, 1, 8, 128), jnp.float32)
    rows = pl.ds(first * 32, frames * 32)
    for v in range(3):
        y = shifted[v].reshape(frames, 4, 8, 128)
        lines = [
            jnp.concatenate([blank, y[:, :3]], axis=1),
            y,
            jnp.concatenate([y[:, 1:], blank], axis=1),
        ]
        for u in range(3):
            tap = u * 3 + v
            target[rows, tap * 128 : (tap + 1) * 128] = (
                lines[u].reshape(frames * 32, 128).astype(jnp.bfloat16)
            )


def body(video, frame_owner, conv_first, conv_second):
    readers = lax.axis_size("clips")
    periods = lax.axis_size("tm")
    slots = video.shape[1]
    cap = max(2, 2 * slots // readers)
    frames = readers * cap
    sizes = (readers, periods, slots, cap)
    vmem = pl.BlockSpec(memory_space=pltpu.VMEM)
    hbm = pl.BlockSpec(memory_space=pltpu.HBM)
    dma = pltpu.SemaphoreType.DMA
    return pl.pallas_call(
        functools.partial(block_kernel, sizes),
        out_shape=jax.ShapeDtypeStruct((1, frames, 4, 8, 64), jnp.bfloat16),
        in_specs=[hbm] * 4,
        out_specs=vmem,
        scratch_shapes=[
            pltpu.VMEM((readers, readers, cap, 16, 128), jnp.bfloat16),
            pltpu.VMEM((readers, cap, 16, 128), jnp.bfloat16),
            pltpu.VMEM((HALO, 32, 128), jnp.bfloat16),
            pltpu.VMEM((HALO, 32, 128), jnp.bfloat16),
            pltpu.VMEM((readers, 1, 128), jnp.int32),
            pltpu.SMEM((readers, 1, 128), jnp.int32),
            pltpu.VMEM((3, 1152, 128), jnp.bfloat16),
            pltpu.VMEM((3, 1152, 128), jnp.bfloat16),
            pltpu.VMEM((frames + HALO, 32, 128), jnp.float32),
            pltpu.VMEM(((frames + HALO) * 32, 1152), jnp.bfloat16),
            pltpu.VMEM(((frames + 2) * 32, 1152), jnp.bfloat16),
            pltpu.VMEM((frames, 32, 64), jnp.float32),
            pltpu.SMEM((1, slots), jnp.int32),
            pltpu.VMEM((slots, 4, 8, 64), jnp.bfloat16),
            pltpu.VMEM((slots, 16, 128), jnp.bfloat16),
            pltpu.SMEM((readers * 32,), jnp.int32),
            dma,
            dma,
            dma,
            dma((2,)),
            dma((readers * readers,)),
            dma((readers * readers,)),
            dma((2 * readers,)),
            dma((readers,)),
            dma((readers,)),
            dma((readers,)),
            dma,
            dma,
        ],
        compiler_params=pltpu.CompilerParams(
            collective_id=0, has_side_effects=True, vmem_limit_bytes=60 * 2**20
        ),
    )(
        video,
        frame_owner.reshape(1, slots),
        conv_first.reshape(3, 1152, 128),
        conv_second.reshape(3, 1152, 128),
    )


def solution(mesh):
    placed = (
        P(("groups", "tm"), "clips", None, None, "chan"),
        P(("groups", "tm"), "clips", None),
        P(),
        P(),
    )
    return jax.shard_map(
        body,
        mesh=mesh,
        in_specs=placed,
        out_specs=P(("groups", "tm"), "clips", None, None, "chan"),
        check_vma=False,
    )
```

time: 19.2 us -> 22.9 us (1.19)
  Pallas kernels: 17.3 us -> 21.1 us
    pallas_call x1, Pallas kernels: 17.3 us -> 21.1 us  [body(): pl.pallas_call(functools.partial(block_kernel, sizes), out_shape=jax.Shap...]
where the time goes in v3:
time: 22.9 us; the launch traced here: 22.8 us
  Pallas kernels  21.1 us (92%)
  local copies, waits for them, and re-layouts  1.67 us (7%)
    pallas_call x1, Pallas kernels, body(): pl.pallas_call(functools.partial(block_kernel, sizes), out_shape=jax.Shap...  21.1 us
    unnamed x1, local copies, waits for them, and re-layouts  1.67 us

profile of v3, /device:TPU:1, one launch (start us, length us, event | category | flops | bytes accessed | tf_op | source)
XLA Modules:
  0.0 22.8 jit_solution(12923867177213546344)
XLA Ops:
  0.0 21.1 %shard_map.46 = bf16[1,32,4,8,64]{4,3,2,1,0:T(8,128)(2,1)} custom-call(bf16[1,16,4,8,64]{4,3,2,1,0:T(8,128)(2,1)} %video.1, s32[1,16]{1,0:T(1,128)} %bitcast.5, bf16[3,1152,128]{2,1,0:T(8,128)(2,1)} %bitcast.3, bf16[3,1152,128]{2,1,0:T(8,128)(2,1)} %bitcast.4), custom_call_target="tpu_custom_call" | custom-call | tf_op jit(solution)/shard_map/pallas_call | solution.py:316
  21.1 1.7 %copy.6 = bf16[1,32,4,8,64]{4,3,2,1,0:T(8,128)(2,1)} copy(bf16[1,32,4,8,64]{4,3,2,1,0:T(8,128)(2,1)} %shard_map.46) | data formatting | bytes 262144

commit v4 on v3

--- a/solution.py
+++ b/solution.py
@@ -41,8 +41,6 @@
         pltpu.make_async_copy(first_in, first, weight_sem.at[0]),
         pltpu.make_async_copy(second_in, second, weight_sem.at[1]),
     ]
-    up = (g, r + 1, p, c)
-    down = (g, r - 1, p, c)
     later = (g, r, p + 1, c)
     earlier = (g, r, p - 1, c)
     sibling = (g, r, p, 1 - c)
@@ -54,8 +52,11 @@
         def _():
             pl.semaphore_signal(barrier, inc=1, device_id=who, device_id_type=MESH)
 
-    greet(r < readers - 1, up)
-    greet(r > 0, down)
+    def greet_clip(i):
+        to = (g, lax.rem(r + i + 1, readers), p, c)
+        pl.semaphore_signal(barrier, inc=1, device_id=to, device_id_type=MESH)
+
+    each(readers - 1, greet_clip)
     greet(p < periods - 1, later)
     greet(p > 0, earlier)
     pl.semaphore_signal(barrier, inc=1, device_id=sibling, device_id_type=MESH)
@@ -94,9 +95,7 @@
 
     each(readers, pack)
     neighbours = (
-        1
-        + jnp.where(r < readers - 1, 1, 0)
-        + jnp.where(r > 0, 1, 0)
+        readers
         + jnp.where(p < periods - 1, 1, 0)
         + jnp.where(p > 0, 1, 0)
     )
@@ -107,12 +106,11 @@
             source, target, sent, got, device_id=who, device_id_type=MESH)
 
     def chunk(s, d, who):
-        at = s * readers + d
-        return remote(box.at[s, d], box.at[s, d], send_sem.at[at], recv_sem.at[at], who)
-
-    def row(s, way, who):
-        return remote(
-            counts.at[s], counts.at[s], count_send.at[2 * s + way], count_recv.at[s], who)
+        to = (g, who, p, c)
+        return (
+            remote(box.at[s, d], box.at[s, d], send_sem.at[d], recv_sem.at[s], to),
+            remote(counts.at[s], counts.at[s], count_send.at[d], count_recv.at[s], to),
+        )
 
     def relay(s):
         return remote(box.at[s, r], other.at[s], pass_send.at[s], pass_recv.at[s], sibling)
@@ -122,55 +120,24 @@
         def _():
             act()
 
-    def start_rows():
-        when(r < readers - 1, lambda: row(r, 0, up).start())
-        when(r > 0, lambda: row(r, 1, down).start())
+    def partner(i):
+        return lax.rem(r + 1 + lax.rem(readers // 2 - 1 + i, readers - 1), readers)
 
     def start_chunks(i):
-        d = readers - 1 - i
-        when(d > r, lambda: chunk(r, d, up).start())
-        when(i < r, lambda: chunk(r, i, down).start())
-
-    each(readers, start_chunks)
-    start_rows()
+        for d in chunk(r, partner(i), partner(i)):
+            d.start()
+
+    each(readers - 1, start_chunks)
     relay(r).start()
 
     def arrive(i):
-        below, above = r - 1 - i, r + 1 + i
-
-        def from_below(j):
-            d = readers - 1 - j
-
-            def take():
-                chunk(below, d, up).wait_recv()
-                when(d > r, lambda: chunk(below, d, up).start())
-                when(d == r, lambda: relay(below).start())
-
-            when((below >= 0) & (d >= r), take)
-
-        def from_above(d):
-            def take():
-                chunk(above, d, down).wait_recv()
-                when(d < r, lambda: chunk(above, d, down).start())
-                when(d == r, lambda: relay(above).start())
-
-            when((above < readers) & (d <= r), take)
-
-        def row_below():
-            row(below, 0, up).wait_recv()
-            when(r < readers - 1, lambda: row(below, 0, up).start())
-
-        def row_above():
-            row(above, 1, down).wait_recv()
-            when(r > 0, lambda: row(above, 1, down).start())
-
-        def both(j):
-            from_below(j)
-            from_above(j)
-
-        each(readers, both)
-        when(below >= 0, row_below)
-        when(above < readers, row_above)
+        def take(s):
+            for d in chunk(s, r, s):
+                d.wait_recv()
+            relay(s).start()
+
+        when(r >= 1 + i, lambda: take(r - 1 - i))
+        when(r + 1 + i < readers, lambda: take(r + 1 + i))
 
     each(readers - 1, arrive)
     known_copy = pltpu.make_async_copy(counts, known, known_sem)
@@ -259,17 +226,12 @@
             y = jnp.where(k < number[q], y, 0.0)
             out[0, q * cap + k] = y.reshape(4, 8, 64).astype(jnp.bfloat16)
 
-    def sent(s):
-        def one(d):
-            when((s <= r) & (d > r), lambda: chunk(s, d, up).wait_send())
-            when((s >= r) & (d < r), lambda: chunk(s, d, down).wait_send())
-
-        each(readers, one)
-        when((s <= r) & (r < readers - 1), lambda: row(s, 0, up).wait_send())
-        when((s >= r) & (r > 0), lambda: row(s, 1, down).wait_send())
-        relay(s).wait_send()
-
-    each(readers, sent)
+    def sent(i):
+        for d in chunk(r, partner(i), partner(i)):
+            d.wait_send()
+
+    each(readers - 1, sent)
+    each(readers, lambda s: relay(s).wait_send())
     when(p < periods - 1, carry.wait_send)
 
 
@@ -339,9 +301,9 @@
             dma,
             dma,
             dma((2,)),
-            dma((readers * readers,)),
-            dma((readers * readers,)),
-            dma((2 * readers,)),
+            dma((readers,)),
+            dma((readers,)),
+            dma((readers,)),
             dma((readers,)),
             dma((readers,)),
             dma((readers,)),

time: 22.9 us -> 18.5 us (0.81)
  Pallas kernels: 21.1 us -> 16.6 us
    pallas_call x1, Pallas kernels: 21.1 us -> 16.6 us  [body(): pl.pallas_call(functools.partial(block_kernel, sizes), out_shape=jax.Shap...]
where the time goes in v4:
time: 18.5 us; the launch traced here: 18.3 us
  Pallas kernels  16.6 us (90%)
  local copies, waits for them, and re-layouts  1.67 us (9%)
    pallas_call x1, Pallas kernels, body(): pl.pallas_call(functools.partial(block_kernel, sizes), out_shape=jax.Shap...  16.6 us
    unnamed x1, local copies, waits for them, and re-layouts  1.67 us

profile of v4, /device:TPU:1, one launch (start us, length us, event | category | flops | bytes accessed | tf_op | source)
XLA Modules:
  0.0 18.3 jit_solution(14101294233963554343)
XLA Ops:
  0.0 16.6 %shard_map.46 = bf16[1,32,4,8,64]{4,3,2,1,0:T(8,128)(2,1)} custom-call(bf16[1,16,4,8,64]{4,3,2,1,0:T(8,128)(2,1)} %video.1, s32[1,16]{1,0:T(1,128)} %bitcast.5, bf16[3,1152,128]{2,1,0:T(8,128)(2,1)} %bitcast.3, bf16[3,1152,128]{2,1,0:T(8,128)(2,1)} %bitcast.4), custom_call_target="tpu_custom_call" | custom-call | tf_op jit(solution)/shard_map/pallas_call | solution.py:278
  16.7 1.7 %copy.6 = bf16[1,32,4,8,64]{4,3,2,1,0:T(8,128)(2,1)} copy(bf16[1,32,4,8,64]{4,3,2,1,0:T(8,128)(2,1)} %shard_map.46) | data formatting | bytes 262144
